TPU v7x, 32 devices: a whole 2x2x4 slice. The times are simulated.
32 devices in a mesh: row: 8 (over y, x, core), col: 4 (over z).
Axes of the slice: x: 2, y: 2, z: 4, core: 2. Of those that a mesh axis runs over, the one named last changes fastest.
Arguments:
- input_feat: bfloat16 [512, 8192], P('row', 'col'), may hold values from -8 to 8
- weight: bfloat16 [512, 512], replicated, may hold values from -0.25 to 0.25
- tile_values: bfloat16 [8, 4, 8, 128, 128], P('row', 'col'), as said below
- tile_slots: int32 [8, 4, 8], P('row', 'col'), may hold values from 0 to 127, as said below
- tile_count: int32 [8, 4], P('row', 'col'), may hold values from 1 to 8, as said below
- grad_output: bfloat16 [512, 8192], P('col', 'row'), may hold values from -8 to 8
Outputs:
- output_feat: bfloat16 [512, 8192], P('col', 'row')
- weight_grad: float32 [512, 512], P('row', 'col')
- grad_input: float32 [512, 8192], P('row', 'col')
Inputs may be any that keep to these rules, and one draw needn't show every extreme that they name: `tile_slots`: in every grid block the 8 entries are distinct tile positions, numbered tile row times 16 plus tile column; only the first tile_count entries of a block are used. `tile_count`: some grid block has all 8 entries live. `tile_values`: entries are zero or positive; most are zero.
All inputs are finite; a program needn't handle non-finite values.
Results may differ from a plain program's by a relative error of at most 0.014.
Values may be sent and summed in bfloat16 or wider, within the bound.
A program may use at most 64 MiB of HBM per device.

v0:
```python
import jax
import jax.numpy as jnp
from jax import lax
from jax.sharding import PartitionSpec as P


def forward_block(values, slots, live_count, columns, row_tiles, loop_count):
    channels = columns.shape[0]
    tile_len = values.shape[-1]
    col_tiles = columns.shape[1] // tile_len
    blocks = columns.reshape(channels, col_tiles, tile_len)

    def forward_add_group(group_idx, running):
        first_tile = group_idx * 8
        is_live = first_tile + jnp.arange(8, dtype=jnp.int32) < live_count
        picked = jnp.take(blocks, slots % col_tiles, axis=1)
        products = jnp.einsum("ftc,trc->tfr", picked, values, preferred_element_type=jnp.float32)
        target = (
            (slots // col_tiles)[:, None] == jnp.arange(row_tiles, dtype=jnp.int32)[None, :]
        ) & is_live[:, None]
        return running + jnp.einsum(
            "tfr,tk->fkr", products, target.astype(jnp.float32), precision=lax.Precision.HIGHEST
        )

    running = lax.fori_loop(
        0, loop_count, forward_add_group, jnp.zeros((channels, row_tiles, tile_len), jnp.float32)
    )
    return running.reshape(channels, row_tiles * tile_len)


def backward_block(values, slots, live_count, rows, col_tiles, loop_count):
    channels = rows.shape[0]
    tile_len = values.shape[-1]
    row_tiles = rows.shape[1] // tile_len
    blocks = rows.reshape(channels, row_tiles, tile_len)

    def backward_add_group(group_idx, running):
        first_tile = group_idx * 8
        is_live = first_tile + jnp.arange(8, dtype=jnp.int32) < live_count
        picked = jnp.take(blocks, slots // col_tiles, axis=1)
        products = jnp.einsum("ftr,trc->tfc", picked, values, preferred_element_type=jnp.float32)
        target = (
            (slots % col_tiles)[:, None] == jnp.arange(col_tiles, dtype=jnp.int32)[None, :]
        ) & is_live[:, None]
        return running + jnp.einsum(
            "tfc,tk->fkc", products, target.astype(jnp.float32), precision=lax.Precision.HIGHEST
        )

    running = lax.fori_loop(
        0, loop_count, backward_add_group, jnp.zeros((channels, col_tiles, tile_len), jnp.float32)
    )
    return running.reshape(channels, col_tiles * tile_len)


def per_device(input_feat, weight, tile_values, tile_slots, tile_count, grad_output):
    values = tile_values[0, 0]
    slots = tile_slots[0, 0]
    live_count = tile_count[0, 0]
    tile_len = values.shape[-1]
    row_tiles = grad_output.shape[1] // tile_len
    col_tiles = input_feat.shape[1] // tile_len
    loop_count = values.shape[0] // 8
    partial_agg = forward_block(
        values,
        slots,
        live_count,
        lax.all_gather(input_feat, "row", axis=0, tiled=True),
        row_tiles,
        loop_count,
    )
    aggregate = lax.psum(partial_agg.astype(jnp.bfloat16), "col")
    out_width = weight.shape[1] // lax.axis_size("col")
    weight_cols = lax.dynamic_slice_in_dim(weight, lax.axis_index("col") * out_width, out_width, 1)
    pre_act = lax.dot_general(
        weight_cols, aggregate, (((0,), (0,)), ((), ())), preferred_element_type=jnp.float32
    )
    sigmoid = jax.nn.sigmoid(pre_act)
    output_feat = (pre_act * sigmoid).astype(jnp.bfloat16)
    grad_pre = (
        grad_output.astype(jnp.float32) * sigmoid * (1.0 + pre_act * (1.0 - sigmoid))
    ).astype(jnp.bfloat16)
    weight_part = lax.dot_general(
        aggregate, grad_pre, (((1,), (1,)), ((), ())), preferred_element_type=jnp.float32
    )
    grad_full = lax.all_gather(grad_pre, "col", axis=0, tiled=True)
    grad_agg = jnp.dot(weight, grad_full, preferred_element_type=jnp.float32).astype(jnp.bfloat16)
    input_part = backward_block(values, slots, live_count, grad_agg, col_tiles, loop_count)
    grad_input, weight_share = (
        lax.psum_scatter(
            input_part.astype(jnp.bfloat16), "row", scatter_dimension=0, tiled=True
        ).astype(jnp.float32),
        lax.psum_scatter(
            weight_part.astype(jnp.bfloat16), "row", scatter_dimension=0, tiled=True
        ).astype(jnp.float32),
    )
    node_total = grad_output.shape[1] * lax.axis_size("row")
    return (output_feat, weight_share * node_total ** (-0.5), grad_input)


def solution(mesh):
    in_specs = (
        P("row", "col"),
        P(),
        P("row", "col", None, None, None),
        P("row", "col", None),
        P("row", "col"),
        P("col", "row"),
    )
    out_specs = (P("col", "row"), P("row", "col"), P("row", "col"))
    return jax.shard_map(
        per_device, mesh=mesh, in_specs=in_specs, out_specs=out_specs, check_vma=False
    )
```

profile of v0, /device:TPU:1, one launch (start us, length us, event | category | flops | bytes accessed | tf_op | source)
XLA Modules:
  0.0 222.4 jit_solution(5726876386773135145)
XLA Ops:
  7.2 0.0 copy-start
  7.2 0.0 all-gather.3.cloned.1.call-start
  7.2 0.7 all-gather.3.cloned.1.call-update
  7.9 0.0 all-reduce.2.cloned.1.call-start
  8.6 0.7 fusion.35
  9.3 0.7 compare_and_fusion
  10.0 30.4 %all-gather.3.cloned.1.call-done = bf16[512,2048]{1,0:T(8,128)(2,1)} async-done(((bf16[64,2048]{1,0:T(8,128)(2,1)}), bf16[512,2048]{1,0:T(8,128)(2,1)}) %all-gather.3.cloned.1.call-update) | async-done | bytes 2097168 | tf_op jit(solution)/shard_map/all_gather | solution.py:67
  40.3 2.9 %copy.14 = bf16[512,2048]{0,1:T(8,128)(2,1)S(1)} copy(bf16[512,2048]{1,0:T(8,128)(2,1)} %all-gather.3.cloned.1.call-done) | data formatting | bytes 4194304 | tf_op jit(solution)/shard_map/all_gather | solution.py:67
  43.2 2.4 %copy.15 = bf16[512,16,128]{2,0,1:T(8,128)(2,1)} copy(bf16[512,16,128]{0,2,1:T(8,128)(2,1)S(1)} %bitcast.78) | data formatting | bytes 4194304 | tf_op jit(solution)/shard_map/reshape | solution.py:11
  45.6 0.0 copy-start.1
  45.6 2.4 %gather_fusion = bf16[8,512,128]{2,1,0:T(8,128)(2,1)S(1)} fusion(bf16[512,16,128]{2,0,1:T(8,128)(2,1)} %copy.15, s32[1024]{0:T(1024)S(1)} %get-tuple-element.56), kind=kCustom, calls=%fused_computation | custom fusion | bytes 2097184 | tf_op jit(solution)/shard_map/while/body/eval_jaxpr/jit(_take)/gather | solution.py:16
  48.0 0.0 copy-done.1
  48.0 0.5 fusion.12
  48.5 2.2 %fusion.7 = bf16[8,512,128]{2,0,1:T(8,128)(2,1)S(1)} fusion(f32[8,512,128]{2,1,0:T(8,128)S(1)} %fusion.12, s32[8]{0:T(128)S(1)} %get-tuple-element.32, pred[8]{0:T(512)(128)(4,1)S(1)} %get-tuple-element.57), kind=kOutput, calls=%fused_computation.8 | convolution fusion | flops 50856064 | bytes 3145768 | tf_op jit(solution)/shard_map/while/body/eval_jaxpr/tfr,tk->fkr/dot_general | solution.py:21
  50.8 0.0 copy-start.3
  50.8 1.3 copy.32
  52.0 0.0 all-reduce.2.cloned.1.call-update
  52.1 0.0 all-gather.5.cloned.1.call-start
  52.1 51.7 %all-reduce.2.cloned.1.call-done = bf16[512,1024]{1,0:T(8,128)(2,1)} async-done(((bf16[512,1024]{1,0:T(8,128)(2,1)}), bf16[512,1024]{1,0:T(8,128)(2,1)}) %all-reduce.2.cloned.1.call-update) | async-done | bytes 1048592 | tf_op jit(solution)/shard_map/psum | solution.py:71
  103.8 0.0 copy-done
  103.8 0.0 copy-done.3
  103.8 0.0 copy-start.2
  103.8 2.6 %multiply_convert_fusion = (bf16[128,1024]{1,0:T(8,128)(2,1)}, bf16[128,1024]{1,0:T(8,128)(2,1)}) fusion(bf16[128,1024]{1,0:T(8,128)(2,1)S(1)} %copy-done.3, bf16[512,1024]{1,0:T(8,128)(2,1)} %all-reduce.2.cloned.1.call-done, bf16[512,512]{1,0:T(8,128)(2,1)S(1)} %copy-done, s32[]{:T(128)S(6)} %select_n.94), kind=kOutput, calls=%fused_computation.22 | convolution fusion | flops 135790592 | bytes 1966084 | tf_op jit(solution)/shard_map/dot_general | solution.py:74
  106.4 0.0 all-gather.5.cloned.1.call-update
  106.5 0.0 reduce-scatter.3.cloned.1.call-start
  106.5 0.0 copy-done.2
  106.5 2.0 convolution_convert_fusion.1
  108.6 0.0 reduce-scatter.3.cloned.1.call-update
  108.6 0.0 reduce-scatter.5.cloned.1.call-start
  108.6 25.0 %all-gather.5.cloned.1.call-done = bf16[512,1024]{1,0:T(8,128)(2,1)} async-done(((bf16[128,1024]{1,0:T(8,128)(2,1)}), bf16[512,1024]{1,0:T(8,128)(2,1)}) %all-gather.5.cloned.1.call-update) | async-done | bytes 1048592 | tf_op jit(solution)/shard_map/all_gather | solution.py:85
  133.6 2.0 convolution_convert_fusion
  135.6 0.7 copy.17
  136.3 0.7 gather_fusion.1
  137.0 0.5 fusion.10
  137.5 4.3 %fusion.4 = bf16[16,512,128]{2,0,1:T(8,128)(2,1)S(1)} fusion(f32[8,512,128]{2,1,0:T(8,128)S(1)} %fusion.10, s32[8]{0:T(128)S(1)} %get-tuple-element.47, pred[8]{0:T(512)(128)(4,1)S(1)} %get-tuple-element.57), kind=kOutput, calls=%fused_computation.7 | convolution fusion | flops 101712128 | bytes 4194344 | tf_op jit(solution)/shard_map/while/body/eval_jaxpr/tfc,tk->fkc/dot_general | solution.py:45
  141.8 1.9 copy.31
  143.7 0.0 reduce-scatter.5.cloned.1.call-update
  143.7 25.6 %reduce-scatter.3.cloned.1.call-done = bf16[64,128]{1,0:T(8,128)(2,1)} async-done(((bf16[512,128]{1,0:T(8,128)(2,1)}), bf16[64,128]{1,0:T(8,128)(2,1)}) %reduce-scatter.3.cloned.1.call-update) | async-done | bytes 16400 | tf_op jit(solution)/shard_map/reduce_scatter | solution.py:92
  169.3 1.3 convert_multiply_fusion
  170.6 43.5 %reduce-scatter.5.cloned.1.call-done = bf16[64,2048]{1,0:T(8,128)(2,1)} async-done(((bf16[512,2048]{1,0:T(8,128)(2,1)}), bf16[64,2048]{1,0:T(8,128)(2,1)}) %reduce-scatter.5.cloned.1.call-update) | async-done | bytes 262160 | tf_op jit(solution)/shard_map/reduce_scatter | solution.py:89
  214.1 1.8 convert_element_type.59
  (1 shorter events, 0.0 us)
Async XLA Ops:
  7.2 96.6 %copy-start = (bf16[512,512]{1,0:T(8,128)(2,1)S(1)}, bf16[512,512]{1,0:T(8,128)(2,1)}, u32[]{:S(2)}) copy-start(bf16[512,512]{1,0:T(8,128)(2,1)} %param.7) | copy-start | bytes 1572868
  7.2 33.2 %all-gather.3.cloned.1.call-start = ((), (), s32[]{:S(2)}) async-start(), calls=%async_computation.2 | async-start | bytes 2359296 | tf_op jit(solution)/shard_map/all_gather | solution.py:67
  7.9 95.9 %all-reduce.2.cloned.1.call-start = ((), (), s32[]{:S(2)}) async-start(), calls=%async_computation.3 | async-start | bytes 2097152 | tf_op jit(solution)/shard_map/psum | solution.py:71
  45.6 2.4 %copy-start.1 = (bf16[1,1,8,128,128]{4,3,2,1,0:T(8,128)(2,1)S(1)}, bf16[1,1,8,128,128]{4,3,2,1,0:T(8,128)(2,1)}, u32[]{:S(2)}) copy-start(bf16[1,1,8,128,128]{4,3,2,1,0:T(8,128)(2,1)} %param.8) | copy-start | bytes 786436
  50.8 53.1 %copy-start.3 = (bf16[128,1024]{1,0:T(8,128)(2,1)S(1)}, bf16[128,1024]{1,0:T(8,128)(2,1)}, u32[]{:S(2)}) copy-start(bf16[128,1024]{1,0:T(8,128)(2,1)} %param.11) | copy-start | bytes 786436
  52.1 81.5 %all-gather.5.cloned.1.call-start = ((), (), s32[]{:S(2)}) async-start(), calls=%async_computation.5 | async-start | bytes 1310720 | tf_op jit(solution)/shard_map/all_gather | solution.py:85
  103.8 2.7 %copy-start.2 = (bf16[512,1024]{1,0:T(8,128)(2,1)S(1)}, bf16[512,1024]{1,0:T(8,128)(2,1)}, u32[]{:S(2)}) copy-start(bf16[512,1024]{1,0:T(8,128)(2,1)} %all-reduce.2.cloned.1.call-done) | copy-start | bytes 3145732
  106.5 62.8 %reduce-scatter.3.cloned.1.call-start = ((), (), s32[]{:S(2)}) async-start(), calls=%async_computation.4 | async-start | bytes 147456 | tf_op jit(solution)/shard_map/reduce_scatter | solution.py:92
  108.6 105.5 %reduce-scatter.5.cloned.1.call-start = ((), (), s32[]{:S(2)}) async-start(), calls=%async_computation.6 | async-start | bytes 2359296 | tf_op jit(solution)/shard_map/reduce_scatter | solution.py:89
Sparse Core Ops, SparseCore 0:
  9.9 30.3 all-gather.2
  52.2 51.5 all-reduce.1
  106.6 26.9 all-gather.4
  136.7 32.4 reduce-scatter.2
  172.4 41.6 reduce-scatter.4
where the time goes:
time: 223 us; the launch traced here: 222 us
  waiting for transfers between devices  177 us (79%)
  between operations  14.5 us (7%)
  matrix products  14.1 us (6%)
  local copies, waits for them, and re-layouts  12.2 us (5%)
  other arithmetic  4.46 us (2%)
    psum x1, waiting for transfers between devices, per_device(): aggregate = lax.psum(partial_agg.astype(jnp.bfloat16), 'col')  51.7 us
    reduce_scatter x1, waiting for transfers between devices, per_device(): lax.psum_scatter(input_part.astype(jnp.bfloat16), 'row', scatter_dimensio...  43.5 us
    all_gather x1, waiting for transfers between devices, per_device(): lax.all_gather(input_feat, 'row', axis=0, tiled=True)  30.4 us
    reduce_scatter x1, waiting for transfers between devices, per_device(): lax.psum_scatter(weight_part.astype(jnp.bfloat16), 'row', scatter_dimensi...  25.6 us
    all_gather x1, waiting for transfers between devices, per_device(): grad_full = lax.all_gather(grad_pre, 'col', axis=0, tiled=True)  25 us
  transfers between devices with their start and end apart: 5, of which 5 were waited for; matrix products, arithmetic and copies ran while one was open for 7% of the time, Pallas kernels for 0%

commit v1 on v0

--- a/solution.py
+++ b/solution.py
@@ -1,7 +1,312 @@
+import functools
+
 import jax
 import jax.numpy as jnp
 from jax import lax
+from jax.experimental import pallas as pl
+from jax.experimental.pallas import tpu as pltpu
 from jax.sharding import PartitionSpec as P
+
+F32, BF16 = jnp.float32, jnp.bfloat16
+
+
+def fused(
+    R, C, x_ref, w_ref, tv_ref, slots_ref, count_ref, go_ref, of_ref, wg_ref, gi_ref,
+    tv_all, xf, pout, prx, agg_s, agg_full, go_full, of_s, of_rx, w_s, w_rx, w2_s, w2_rx,
+    ga_s, ga_rx, ga_all,
+    sdir, sfwd, rtv, sgo, rgo, szr, rzr, sa, ra, sof, rof, swz, rwz, swr, rwr, sg, rg, sgz, rgz,
+):
+    T, L = tv_ref.shape[2], tv_ref.shape[3]
+    FR, NB = x_ref.shape
+    FC, NR = go_ref.shape
+    F = w_ref.shape[0]
+    RT, CT, SH = NR // L, NB // L, NR // C
+    per = SH // L
+    mi, mj = lax.axis_index("row"), lax.axis_index("col")
+    sib = mi + 1 - 2 * lax.rem(mi, 2)
+    half = R // 2
+
+    def rowp(p):
+        return {"row": p}
+
+    def colp(p):
+        return {"col": p}
+
+    def rcopy(src, dst, ss, rs, dev):
+        return pltpu.make_async_remote_copy(
+            src_ref=src, dst_ref=dst, send_sem=ss, recv_sem=rs, device_id=dev,
+            device_id_type=pl.DeviceIdType.MESH,
+        )
+
+    def rows(d):
+        return lax.rem(mi + d, R)
+
+    def cols(d):
+        return lax.rem(mj + d, C)
+
+    barrier = pltpu.get_barrier_semaphore()
+    for d in range(1, R):
+        pl.semaphore_signal(barrier, inc=1, device_id=rowp(rows(d)), device_id_type=pl.DeviceIdType.MESH)
+    for d in range(1, C):
+        pl.semaphore_signal(barrier, inc=1, device_id=colp(cols(d)), device_id_type=pl.DeviceIdType.MESH)
+
+    tv_all[mi, 0 : T * L, :] = tv_ref[0, 0].reshape(T * L, L)
+    count = count_ref[0, 0]
+    lines = []
+    for t in range(T):
+        lines.append(jnp.full((1, L), lax.rem(slots_ref[0, 0, t], CT), jnp.int32))
+    for t in range(T):
+        home = jnp.where(t < count, lax.div(slots_ref[0, 0, t], CT), RT)
+        lines.append(jnp.full((1, L), home, jnp.int32))
+    tv_all[mi, T * L : T * L + 2 * T, :] = jnp.concatenate(lines, axis=0).astype(F32).astype(BF16)
+    xf[...] = x_ref[...].astype(F32)
+
+    pl.semaphore_wait(barrier, R + C - 2)
+
+    for m in range(1, half):
+        rcopy(tv_all.at[mi], tv_all.at[mi], sdir.at[m], rtv.at[mi], rowp(rows(2 * m))).start()
+    for d in range(1, C):
+        rcopy(
+            go_ref.at[:, pl.ds(pl.multiple_of(cols(d) * SH, SH), SH)],
+            go_full.at[mj], sgo.at[d], rgo.at[mj], colp(cols(d)),
+        ).start()
+    go_full[mj] = go_ref[:, pl.ds(pl.multiple_of(mj * SH, SH), SH)]
+
+    def forward(b):
+        info = tv_all[b, T * L : T * L + 2 * T, :].astype(F32)
+        prods = []
+        for t in range(T):
+            colv = jnp.broadcast_to(info[t : t + 1, :], (FR, L))
+            pick = jnp.zeros((FR, L), F32)
+            for c in range(CT):
+                pick = jnp.where(colv == c, xf[:, c * L : (c + 1) * L], pick)
+            prods.append(
+                lax.dot_general(
+                    pick.astype(BF16), tv_all[b, t * L : (t + 1) * L, :],
+                    (((1,), (1,)), ((), ())), preferred_element_type=F32,
+                )
+            )
+        for k in range(RT):
+            acc = jnp.zeros((FR, L), F32)
+            for t in range(T):
+                rowv = jnp.broadcast_to(info[T + t : T + t + 1, :], (FR, L))
+                acc = acc + jnp.where(rowv == k, prods[t], 0.0)
+            pout[k // per, b, :, (k % per) * L : (k % per + 1) * L] = acc.astype(BF16)
+        for d in range(1, C):
+            rcopy(
+                pout.at[cols(d), b], prx.at[mj, b], szr.at[b, d], rzr.at[b, mj], colp(cols(d))
+            ).start()
+
+    def wait_tv(b):
+        rcopy(tv_all.at[b], tv_all.at[b], sfwd.at[0], rtv.at[b], rowp(sib)).wait_recv()
+
+    def gather_step(m, carry):
+        p, q = rows(2 * m), lax.rem(sib + 2 * m, R)
+
+        @pl.when(m > 0)
+        def _():
+            wait_tv(p)
+
+        rcopy(tv_all.at[p], tv_all.at[p], sfwd.at[m], rtv.at[p], rowp(sib)).start()
+
+        def one(h, carry):
+            b = jnp.where(h == 0, p, q)
+
+            @pl.when(h == 1)
+            def _():
+                wait_tv(q)
+
+            forward(b)
+            return carry
+
+        return lax.fori_loop(0, 2, one, carry)
+
+    lax.fori_loop(0, half, gather_step, 0)
+
+    def reduce_step(n, carry):
+        m, h = lax.div(n, 2), lax.rem(n, 2)
+        b = lax.rem(jnp.where(h == 0, mi, sib) + 2 * m, R)
+        total = pout[mj, b].astype(F32)
+        for d in range(1, C):
+            rcopy(pout.at[cols(d), b], prx.at[cols(d), b], szr.at[b, d], rzr.at[b, cols(d)], colp(cols(d))).wait_recv()
+            total = total + prx[cols(d), b].astype(F32)
+        agg_s[b] = total.astype(BF16)
+
+        @pl.when(b == mi)
+        def _():
+            agg_full[mi] = agg_s[mi]
+
+        @pl.when(b != mi)
+        def _():
+            rcopy(agg_s.at[b], agg_full.at[mi], sa.at[b], ra.at[mi], rowp(b)).start()
+
+        return carry
+
+    lax.fori_loop(0, R, reduce_step, 0)
+
+    for d in range(1, C):
+        rcopy(go_full.at[cols(d)], go_full.at[cols(d)], sgo.at[d], rgo.at[cols(d)], colp(cols(d))).wait_recv()
+    for d in range(1, R):
+        p = rows(d)
+        rcopy(agg_s.at[p], agg_full.at[p], sa.at[p], ra.at[p], rowp(p)).wait_recv()
+
+    agg = agg_full[...].reshape(F, SH)
+    pre = lax.dot_general(w_ref[...], agg, (((0,), (0,)), ((), ())), preferred_element_type=F32)
+    s = 1.0 / (1.0 + jnp.exp(-pre))
+    gp = (go_full[...].reshape(F, SH).astype(F32) * s * (1.0 + pre * (1.0 - s))).astype(BF16)
+    ga_s[...] = jnp.dot(w_ref[...], gp, preferred_element_type=F32).astype(BF16).reshape(R, FR, SH)
+    for d in range(1, R):
+        p = rows(d)
+        rcopy(ga_s.at[p], ga_rx.at[mi], sg.at[p], rg.at[mi], rowp(p)).start()
+    of_s[...] = (pre * s).astype(BF16).reshape(C, FC, SH)
+    ga_rx[mi] = ga_s[mi]
+
+    def spread(n, carry):
+        p = rows(n)
+
+        @pl.when(n > 0)
+        def _():
+            rcopy(ga_s.at[p], ga_rx.at[p], sg.at[p], rg.at[p], rowp(p)).wait_recv()
+
+        for d in range(1, C):
+            rcopy(ga_rx.at[p], ga_all.at[mj, p], sgz.at[p, d], rgz.at[p, mj], colp(cols(d))).start()
+        ga_all[mj, p] = ga_rx[p]
+        return carry
+
+    lax.fori_loop(0, R, spread, 0)
+
+    for j in range(C):
+        w_s[j] = lax.dot_general(
+            agg, gp[j * FC : (j + 1) * FC, :], (((1,), (1,)), ((), ())), preferred_element_type=F32
+        ).astype(BF16)
+    for d in range(1, C):
+        q = cols(d)
+        rcopy(w_s.at[q], w_rx.at[mj], swz.at[d], rwz.at[mj], colp(q)).start()
+        rcopy(of_s.at[q], of_rx.at[mj], sof.at[d], rof.at[mj], colp(q)).start()
+    of_rx[mj] = of_s[mj]
+
+    gi_ref[...] = jnp.zeros_like(gi_ref)
+
+    def backward(n, carry):
+        b = rows(n)
+        for d in range(1, C):
+            q = cols(d)
+            rcopy(ga_rx.at[b], ga_all.at[q, b], sgz.at[b, d], rgz.at[b, q], colp(q)).wait_recv()
+        info = tv_all[b, T * L : T * L + 2 * T, :].astype(F32)
+        prods = []
+        for t in range(T):
+            rowv = jnp.broadcast_to(info[T + t : T + t + 1, :], (FR, L))
+            pick = jnp.zeros((FR, L), F32)
+            for k in range(RT):
+                part = ga_all[k // per, b, :, (k % per) * L : (k % per + 1) * L].astype(F32)
+                pick = jnp.where(rowv == k, part, pick)
+            prods.append(
+                jnp.dot(pick.astype(BF16), tv_all[b, t * L : (t + 1) * L, :], preferred_element_type=F32)
+            )
+        for c in range(CT):
+            acc = gi_ref[:, c * L : (c + 1) * L]
+            for t in range(T):
+                colv = jnp.broadcast_to(info[t : t + 1, :], (FR, L))
+                acc = acc + jnp.where(colv == c, prods[t], 0.0)
+            gi_ref[:, c * L : (c + 1) * L] = acc
+        return carry
+
+    lax.fori_loop(0, R, backward, 0)
+
+    total = w_s[mj].astype(F32)
+    for d in range(1, C):
+        q = cols(d)
+        rcopy(w_s.at[q], w_rx.at[q], swz.at[d], rwz.at[q], colp(q)).wait_recv()
+        total = total + w_rx[q].astype(F32)
+    w2_s[...] = total.astype(BF16).reshape(R, FR, FC)
+    for d in range(1, R):
+        p = rows(d)
+        rcopy(w2_s.at[p], w2_rx.at[mi], swr.at[p], rwr.at[mi], rowp(p)).start()
+    for d in range(1, C):
+        q = cols(d)
+        rcopy(of_s.at[q], of_rx.at[q], sof.at[d], rof.at[q], colp(q)).wait_recv()
+    for j in range(C):
+        of_ref[:, j * SH : (j + 1) * SH] = of_rx[j]
+    total = w2_s[mi].astype(F32)
+    for d in range(1, R):
+        p = rows(d)
+        rcopy(w2_s.at[p], w2_rx.at[p], swr.at[p], rwr.at[p], rowp(p)).wait_recv()
+        total = total + w2_rx[p].astype(F32)
+    wg_ref[...] = total * (NR * R) ** -0.5
+
+    for m in range(1, half):
+        rcopy(tv_all.at[mi], tv_all.at[mi], sdir.at[m], rtv.at[mi], rowp(rows(2 * m))).wait_send()
+    for m in range(half):
+        rcopy(tv_all.at[mi], tv_all.at[mi], sfwd.at[m], rtv.at[mi], rowp(sib)).wait_send()
+    for d in range(1, C):
+        q = cols(d)
+        rcopy(go_full.at[mj], go_full.at[mj], sgo.at[d], rgo.at[mj], colp(q)).wait_send()
+        rcopy(w_s.at[q], w_rx.at[mj], swz.at[d], rwz.at[mj], colp(q)).wait_send()
+        rcopy(of_s.at[q], of_rx.at[mj], sof.at[d], rof.at[mj], colp(q)).wait_send()
+
+    def drain(n, carry):
+        p = rows(n)
+        for d in range(1, C):
+            q = cols(d)
+            rcopy(pout.at[q, p], prx.at[mj, p], szr.at[p, d], rzr.at[p, mj], colp(q)).wait_send()
+            rcopy(ga_rx.at[p], ga_all.at[mj, p], sgz.at[p, d], rgz.at[p, mj], colp(q)).wait_send()
+
+        @pl.when(n > 0)
+        def _():
+            rcopy(agg_s.at[p], agg_full.at[mi], sa.at[p], ra.at[mi], rowp(p)).wait_send()
+            rcopy(ga_s.at[p], ga_rx.at[mi], sg.at[p], rg.at[mi], rowp(p)).wait_send()
+            rcopy(w2_s.at[p], w2_rx.at[mi], swr.at[p], rwr.at[mi], rowp(p)).wait_send()
+
+        return carry
+
+    lax.fori_loop(0, R, drain, 0)
+
+
+def fused_device(R, C, x, w, tv, slots, count, go):
+    T, L = tv.shape[2], tv.shape[3]
+    FR, NB = x.shape
+    FC, NR = go.shape
+    F, SH = w.shape[0], NR // C
+    vm, dma = pltpu.VMEM, pltpu.SemaphoreType.DMA
+    scratch = [
+        vm((R, T * L + 2 * T, L), BF16), vm((FR, NB), F32),
+        vm((C, R, FR, SH), BF16), vm((C, R, FR, SH), BF16),
+        vm((R, FR, SH), BF16), vm((R, FR, SH), BF16), vm((C, FC, SH), BF16),
+        vm((C, FC, SH), BF16), vm((C, FC, SH), BF16),
+        vm((C, F, FC), BF16), vm((C, F, FC), BF16),
+        vm((R, FR, FC), BF16), vm((R, FR, FC), BF16),
+        vm((R, FR, SH), BF16), vm((R, FR, SH), BF16), vm((C, R, FR, SH), BF16),
+        dma((R // 2,)), dma((R // 2,)), dma((R,)), dma((C,)), dma((C,)),
+        dma((R, C)), dma((R, C)), dma((R,)), dma((R,)), dma((C,)), dma((C,)),
+        dma((C,)), dma((C,)), dma((R,)), dma((R,)), dma((R,)), dma((R,)), dma((R, C)), dma((R, C)),
+    ]
+    vmem, smem = pl.BlockSpec(memory_space=pltpu.VMEM), pl.BlockSpec(memory_space=pltpu.SMEM)
+    return pl.pallas_call(
+        functools.partial(fused, R, C),
+        out_shape=(
+            jax.ShapeDtypeStruct((FC, NR), BF16),
+            jax.ShapeDtypeStruct((FR, FC), F32),
+            jax.ShapeDtypeStruct((FR, NB), F32),
+        ),
+        in_specs=[vmem, vmem, vmem, smem, smem, vmem],
+        out_specs=(vmem, vmem, vmem),
+        scratch_shapes=scratch,
+        compiler_params=pltpu.CompilerParams(
+            collective_id=0, has_side_effects=True, vmem_limit_bytes=40 * 1024 * 1024
+        ),
+    )(x, w, tv, slots, count, go)
+
+
+def gather(x, axis):
+    n = lax.axis_size(axis)
+    spread = jnp.broadcast_to(x[None], (n,) + x.shape)
+    return lax.all_to_all(spread, axis, 0, 0).reshape((n * x.shape[0],) + x.shape[1:])
+
+
+def scatter_sum(x, axis):
+    n = lax.axis_size(axis)
+    parts = lax.all_to_all(x.reshape((n, x.shape[0] // n) + x.shape[1:]), axis, 0, 0)
+    return jnp.sum(parts.astype(F32), axis=0)
 
 
 def forward_block(values, slots, live_count, columns, row_tiles, loop_count):
@@ -64,11 +369,11 @@
         values,
         slots,
         live_count,
-        lax.all_gather(input_feat, "row", axis=0, tiled=True),
+        gather(input_feat, "row"),
         row_tiles,
         loop_count,
     )
-    aggregate = lax.psum(partial_agg.astype(jnp.bfloat16), "col")
+    aggregate = gather(scatter_sum(partial_agg.astype(jnp.bfloat16), "col").astype(jnp.bfloat16), "col")
     out_width = weight.shape[1] // lax.axis_size("col")
     weight_cols = lax.dynamic_slice_in_dim(weight, lax.axis_index("col") * out_width, out_width, 1)
     pre_act = lax.dot_general(
@@ -82,17 +387,11 @@
     weight_part = lax.dot_general(
         aggregate, grad_pre, (((1,), (1,)), ((), ())), preferred_element_type=jnp.float32
     )
-    grad_full = lax.all_gather(grad_pre, "col", axis=0, tiled=True)
+    grad_full = gather(grad_pre, "col")
     grad_agg = jnp.dot(weight, grad_full, preferred_element_type=jnp.float32).astype(jnp.bfloat16)
     input_part = backward_block(values, slots, live_count, grad_agg, col_tiles, loop_count)
-    grad_input, weight_share = (
-        lax.psum_scatter(
-            input_part.astype(jnp.bfloat16), "row", scatter_dimension=0, tiled=True
-        ).astype(jnp.float32),
-        lax.psum_scatter(
-            weight_part.astype(jnp.bfloat16), "row", scatter_dimension=0, tiled=True
-        ).astype(jnp.float32),
-    )
+    grad_input = scatter_sum(input_part.astype(jnp.bfloat16), "row")
+    weight_share = scatter_sum(weight_part.astype(jnp.bfloat16), "row")
     node_total = grad_output.shape[1] * lax.axis_size("row")
     return (output_feat, weight_share * node_total ** (-0.5), grad_input)
 
@@ -107,6 +406,13 @@
         P("col", "row"),
     )
     out_specs = (P("col", "row"), P("row", "col"), P("row", "col"))
+    R, C = mesh.shape["row"], mesh.shape["col"]
+
+    def device(x, w, tv, slots, count, go):
+        if R % 2 == 0 and go.shape[1] % (C * tv.shape[-1]) == 0 and x.shape[0] % 16 == 0:
+            return fused_device(R, C, x, w, tv, slots, count, go)
+        return per_device(x, w, tv, slots, count, go)
+
     return jax.shard_map(
-        per_device, mesh=mesh, in_specs=in_specs, out_specs=out_specs, check_vma=False
-    )
+        device, mesh=mesh, in_specs=in_specs, out_specs=out_specs, check_vma=False
+    )

time: 223 us -> 93.2 us (0.42)
  the two profiles are of different devices: /device:TPU:1 before, /device:TPU:25 now
where the time goes in v1:
time: 93.2 us; the launch traced here: 92.9 us
  Pallas kernels  85.6 us (92%)
  local copies, waits for them, and re-layouts  6 us (6%)
  between operations  1.33 us (1%)
    pallas_call x1, Pallas kernels, fused_device(): pl.pallas_call(functools.partial(fused, R, C), out_shape=(jax.ShapeDtypeS...  85.6 us
    unnamed x13, local copies, waits for them, and re-layouts  6 us

profile of v1, /device:TPU:25, one launch (start us, length us, event | category | flops | bytes accessed | tf_op | source)
XLA Modules:
  0.0 92.9 jit_solution(15381887344967400099)
XLA Ops:
  0.6 0.0 copy-start.4
  1.3 0.0 copy-done.4
  1.3 0.0 copy-start
  1.3 1.0 %copy-done = bf16[512,512]{1,0:T(8,128)(2,1)S(1)} copy-done((bf16[512,512]{1,0:T(8,128)(2,1)S(1)}, bf16[512,512]{1,0:T(8,128)(2,1)}, u32[]{:S(2)}) %copy-start) | copy-done | bytes 524312
  2.4 0.0 copy-start.1
  2.4 0.9 %copy-done.1 = bf16[64,2048]{1,0:T(8,128)(2,1)S(1)} copy-done((bf16[64,2048]{1,0:T(8,128)(2,1)S(1)}, bf16[64,2048]{1,0:T(8,128)(2,1)}, u32[]{:S(2)}) %copy-start.1) | copy-done | bytes 262168
  3.3 0.0 copy-start.2
  3.3 0.9 %copy-done.2 = bf16[1,1,8,128,128]{4,3,2,1,0:T(8,128)(2,1)S(1)} copy-done((bf16[1,1,8,128,128]{4,3,2,1,0:T(8,128)(2,1)S(1)}, bf16[1,1,8,128,128]{4,3,2,1,0:T(8,128)(2,1)}, u32[]{:S(2)}) %copy-start.2) | copy-done | bytes 262168
  4.3 0.0 copy-start.3
  4.3 0.9 %copy-done.3 = bf16[128,1024]{1,0:T(8,128)(2,1)S(1)} copy-done((bf16[128,1024]{1,0:T(8,128)(2,1)S(1)}, bf16[128,1024]{1,0:T(8,128)(2,1)}, u32[]{:S(2)}) %copy-start.3) | copy-done | bytes 262168
  5.2 85.6 %shard_map.85 = (bf16[128,1024]{1,0:T(8,128)(2,1)S(1)}, f32[64,128]{1,0:T(8,128)S(1)}, f32[64,2048]{1,0:T(8,128)S(1)}) custom-call(bf16[64,2048]{1,0:T(8,128)(2,1)S(1)} %copy-done.1, bf16[512,512]{1,0:T(8,128)(2,1)S(1)} %copy-done, bf16[1,1,8,128,128]{4,3,2,1,0:T(8,128)(2,1)S(1)} %copy-done.2, s32[1,1,8]{2,1,0:T(1,128)S(1)} %copy-done.4, ...), custom_call_target="tpu_custom_call" | custom-call | tf_op jit(solution)/shard_map/pallas_call | solution.py:284
  90.8 0.7 copy.13
  91.5 0.6 copy.14
  92.1 0.8 copy.15
Async XLA Ops:
  0.6 0.7 copy-start.4
  1.3 1.0 %copy-start = (bf16[512,512]{1,0:T(8,128)(2,1)S(1)}, bf16[512,512]{1,0:T(8,128)(2,1)}, u32[]{:S(2)}) copy-start(bf16[512,512]{1,0:T(8,128)(2,1)} %w_ref.1) | copy-start | bytes 1572868
  2.4 0.9 %copy-start.1 = (bf16[64,2048]{1,0:T(8,128)(2,1)S(1)}, bf16[64,2048]{1,0:T(8,128)(2,1)}, u32[]{:S(2)}) copy-start(bf16[64,2048]{1,0:T(8,128)(2,1)} %x_ref.1) | copy-start | bytes 786436
  3.3 0.9 %copy-start.2 = (bf16[1,1,8,128,128]{4,3,2,1,0:T(8,128)(2,1)S(1)}, bf16[1,1,8,128,128]{4,3,2,1,0:T(8,128)(2,1)}, u32[]{:S(2)}) copy-start(bf16[1,1,8,128,128]{4,3,2,1,0:T(8,128)(2,1)} %tv_ref.1) | copy-start | bytes 786436
  4.3 0.9 %copy-start.3 = (bf16[128,1024]{1,0:T(8,128)(2,1)S(1)}, bf16[128,1024]{1,0:T(8,128)(2,1)}, u32[]{:S(2)}) copy-start(bf16[128,1024]{1,0:T(8,128)(2,1)} %go_ref.1) | copy-start | bytes 786436

commit v2 on v1

--- a/solution.py
+++ b/solution.py
@@ -11,12 +11,13 @@
 
 
 def fused(
-    R, C, x_ref, w_ref, tv_ref, slots_ref, count_ref, go_ref, of_ref, wg_ref, gi_ref,
+    R, C, T, x_hbm, w_hbm, tv_hbm, slots_ref, count_ref, go_hbm, of_ref, wg_ref, gi_ref,
+    x_ref, w_ref, go_ref, lsem,
     tv_all, xf, pout, prx, agg_s, agg_full, go_full, of_s, of_rx, w_s, w_rx, w2_s, w2_rx,
     ga_s, ga_rx, ga_all,
     sdir, sfwd, rtv, sgo, rgo, szr, rzr, sa, ra, sof, rof, swz, rwz, swr, rwr, sg, rg, sgz, rgz,
 ):
-    T, L = tv_ref.shape[2], tv_ref.shape[3]
+    L = tv_hbm.shape[1]
     FR, NB = x_ref.shape
     FC, NR = go_ref.shape
     F = w_ref.shape[0]
@@ -44,13 +45,21 @@
     def cols(d):
         return lax.rem(mj + d, C)
 
+    loads = [
+        pltpu.make_async_copy(tv_hbm, tv_all.at[mi, 0 : T * L], lsem.at[0]),
+        pltpu.make_async_copy(go_hbm, go_ref, lsem.at[1]),
+        pltpu.make_async_copy(x_hbm, x_ref, lsem.at[2]),
+        pltpu.make_async_copy(w_hbm, w_ref, lsem.at[3]),
+    ]
+    for load in loads:
+        load.start()
+
     barrier = pltpu.get_barrier_semaphore()
     for d in range(1, R):
         pl.semaphore_signal(barrier, inc=1, device_id=rowp(rows(d)), device_id_type=pl.DeviceIdType.MESH)
     for d in range(1, C):
         pl.semaphore_signal(barrier, inc=1, device_id=colp(cols(d)), device_id_type=pl.DeviceIdType.MESH)
 
-    tv_all[mi, 0 : T * L, :] = tv_ref[0, 0].reshape(T * L, L)
     count = count_ref[0, 0]
     lines = []
     for t in range(T):
@@ -59,9 +68,9 @@
         home = jnp.where(t < count, lax.div(slots_ref[0, 0, t], CT), RT)
         lines.append(jnp.full((1, L), home, jnp.int32))
     tv_all[mi, T * L : T * L + 2 * T, :] = jnp.concatenate(lines, axis=0).astype(F32).astype(BF16)
-    xf[...] = x_ref[...].astype(F32)
-
     pl.semaphore_wait(barrier, R + C - 2)
+    loads[0].wait()
+    loads[1].wait()
 
     for m in range(1, half):
         rcopy(tv_all.at[mi], tv_all.at[mi], sdir.at[m], rtv.at[mi], rowp(rows(2 * m))).start()
@@ -71,6 +80,9 @@
             go_full.at[mj], sgo.at[d], rgo.at[mj], colp(cols(d)),
         ).start()
     go_full[mj] = go_ref[:, pl.ds(pl.multiple_of(mj * SH, SH), SH)]
+
+    loads[2].wait()
+    xf[...] = x_ref[...].astype(F32)
 
     def forward(b):
         info = tv_all[b, T * L : T * L + 2 * T, :].astype(F32)
@@ -150,6 +162,7 @@
         p = rows(d)
         rcopy(agg_s.at[p], agg_full.at[p], sa.at[p], ra.at[p], rowp(p)).wait_recv()
 
+    loads[3].wait()
     agg = agg_full[...].reshape(F, SH)
     pre = lax.dot_general(w_ref[...], agg, (((0,), (0,)), ((), ())), preferred_element_type=F32)
     s = 1.0 / (1.0 + jnp.exp(-pre))
@@ -175,15 +188,27 @@
 
     lax.fori_loop(0, R, spread, 0)
 
-    for j in range(C):
-        w_s[j] = lax.dot_general(
-            agg, gp[j * FC : (j + 1) * FC, :], (((1,), (1,)), ((), ())), preferred_element_type=F32
-        ).astype(BF16)
+    w_s[...] = lax.dot_general(
+        agg, gp, (((1,), (1,)), ((), ())), preferred_element_type=F32
+    ).astype(BF16).reshape(R, FR, F)
+    for d in range(1, R):
+        p = rows(d)
+        rcopy(w_s.at[p], w_rx.at[mi], swr.at[p], rwr.at[mi], rowp(p)).start()
     for d in range(1, C):
         q = cols(d)
-        rcopy(w_s.at[q], w_rx.at[mj], swz.at[d], rwz.at[mj], colp(q)).start()
         rcopy(of_s.at[q], of_rx.at[mj], sof.at[d], rof.at[mj], colp(q)).start()
     of_rx[mj] = of_s[mj]
+
+    total = w_s[mi].astype(F32)
+    for d in range(1, R):
+        p = rows(d)
+        rcopy(w_s.at[p], w_rx.at[p], swr.at[p], rwr.at[p], rowp(p)).wait_recv()
+        total = total + w_rx[p].astype(F32)
+    for j in range(C):
+        w2_s[j] = total[:, j * FC : (j + 1) * FC].astype(BF16)
+    for d in range(1, C):
+        q = cols(d)
+        rcopy(w2_s.at[q], w2_rx.at[mj], swz.at[d], rwz.at[mj], colp(q)).start()
 
     gi_ref[...] = jnp.zeros_like(gi_ref)
 
@@ -213,25 +238,16 @@
 
     lax.fori_loop(0, R, backward, 0)
 
-    total = w_s[mj].astype(F32)
-    for d in range(1, C):
-        q = cols(d)
-        rcopy(w_s.at[q], w_rx.at[q], swz.at[d], rwz.at[q], colp(q)).wait_recv()
-        total = total + w_rx[q].astype(F32)
-    w2_s[...] = total.astype(BF16).reshape(R, FR, FC)
-    for d in range(1, R):
-        p = rows(d)
-        rcopy(w2_s.at[p], w2_rx.at[mi], swr.at[p], rwr.at[mi], rowp(p)).start()
     for d in range(1, C):
         q = cols(d)
         rcopy(of_s.at[q], of_rx.at[q], sof.at[d], rof.at[q], colp(q)).wait_recv()
     for j in range(C):
         of_ref[:, j * SH : (j + 1) * SH] = of_rx[j]
-    total = w2_s[mi].astype(F32)
-    for d in range(1, R):
-        p = rows(d)
-        rcopy(w2_s.at[p], w2_rx.at[p], swr.at[p], rwr.at[p], rowp(p)).wait_recv()
-        total = total + w2_rx[p].astype(F32)
+    total = w2_s[mj].astype(F32)
+    for d in range(1, C):
+        q = cols(d)
+        rcopy(w2_s.at[q], w2_rx.at[q], swz.at[d], rwz.at[q], colp(q)).wait_recv()
+        total = total + w2_rx[q].astype(F32)
     wg_ref[...] = total * (NR * R) ** -0.5
 
     for m in range(1, half):
@@ -241,7 +257,7 @@
     for d in range(1, C):
         q = cols(d)
         rcopy(go_full.at[mj], go_full.at[mj], sgo.at[d], rgo.at[mj], colp(q)).wait_send()
-        rcopy(w_s.at[q], w_rx.at[mj], swz.at[d], rwz.at[mj], colp(q)).wait_send()
+        rcopy(w2_s.at[q], w2_rx.at[mj], swz.at[d], rwz.at[mj], colp(q)).wait_send()
         rcopy(of_s.at[q], of_rx.at[mj], sof.at[d], rof.at[mj], colp(q)).wait_send()
 
     def drain(n, carry):
@@ -255,7 +271,7 @@
         def _():
             rcopy(agg_s.at[p], agg_full.at[mi], sa.at[p], ra.at[mi], rowp(p)).wait_send()
             rcopy(ga_s.at[p], ga_rx.at[mi], sg.at[p], rg.at[mi], rowp(p)).wait_send()
-            rcopy(w2_s.at[p], w2_rx.at[mi], swr.at[p], rwr.at[mi], rowp(p)).wait_send()
+            rcopy(w_s.at[p], w_rx.at[mi], swr.at[p], rwr.at[mi], rowp(p)).wait_send()
 
         return carry
 
@@ -269,32 +285,34 @@
     F, SH = w.shape[0], NR // C
     vm, dma = pltpu.VMEM, pltpu.SemaphoreType.DMA
     scratch = [
+        vm((FR, NB), BF16), vm((F, F), BF16), vm((FC, NR), BF16), dma((4,)),
         vm((R, T * L + 2 * T, L), BF16), vm((FR, NB), F32),
         vm((C, R, FR, SH), BF16), vm((C, R, FR, SH), BF16),
         vm((R, FR, SH), BF16), vm((R, FR, SH), BF16), vm((C, FC, SH), BF16),
         vm((C, FC, SH), BF16), vm((C, FC, SH), BF16),
-        vm((C, F, FC), BF16), vm((C, F, FC), BF16),
-        vm((R, FR, FC), BF16), vm((R, FR, FC), BF16),
+        vm((R, FR, F), BF16), vm((R, FR, F), BF16),
+        vm((C, FR, FC), BF16), vm((C, FR, FC), BF16),
         vm((R, FR, SH), BF16), vm((R, FR, SH), BF16), vm((C, R, FR, SH), BF16),
         dma((R // 2,)), dma((R // 2,)), dma((R,)), dma((C,)), dma((C,)),
         dma((R, C)), dma((R, C)), dma((R,)), dma((R,)), dma((C,)), dma((C,)),
         dma((C,)), dma((C,)), dma((R,)), dma((R,)), dma((R,)), dma((R,)), dma((R, C)), dma((R, C)),
     ]
     vmem, smem = pl.BlockSpec(memory_space=pltpu.VMEM), pl.BlockSpec(memory_space=pltpu.SMEM)
+    hbm = pl.BlockSpec(memory_space=pltpu.HBM)
     return pl.pallas_call(
-        functools.partial(fused, R, C),
+        functools.partial(fused, R, C, T),
         out_shape=(
             jax.ShapeDtypeStruct((FC, NR), BF16),
             jax.ShapeDtypeStruct((FR, FC), F32),
             jax.ShapeDtypeStruct((FR, NB), F32),
         ),
-        in_specs=[vmem, vmem, vmem, smem, smem, vmem],
+        in_specs=[hbm, hbm, hbm, smem, smem, hbm],
         out_specs=(vmem, vmem, vmem),
         scratch_shapes=scratch,
         compiler_params=pltpu.CompilerParams(
-            collective_id=0, has_side_effects=True, vmem_limit_bytes=40 * 1024 * 1024
+            collective_id=0, has_side_effects=True, vmem_limit_bytes=60 * 1024 * 1024
         ),
-    )(x, w, tv, slots, count, go)
+    )(x, w, tv.reshape(T * L, L), slots, count, go)
 
 
 def gather(x, axis):
@@ -307,6 +325,11 @@
     n = lax.axis_size(axis)
     parts = lax.all_to_all(x.reshape((n, x.shape[0] // n) + x.shape[1:]), axis, 0, 0)
     return jnp.sum(parts.astype(F32), axis=0)
+
+
+def pick_blocks(blocks, index):
+    chosen = index[:, None] == jnp.arange(blocks.shape[1], dtype=jnp.int32)[None, :]
+    return jnp.einsum("fkc,tk->ftc", blocks, chosen.astype(blocks.dtype))
 
 
 def forward_block(values, slots, live_count, columns, row_tiles, loop_count):
@@ -318,7 +341,7 @@
     def forward_add_group(group_idx, running):
         first_tile = group_idx * 8
         is_live = first_tile + jnp.arange(8, dtype=jnp.int32) < live_count
-        picked = jnp.take(blocks, slots % col_tiles, axis=1)
+        picked = pick_blocks(blocks, slots % col_tiles)
         products = jnp.einsum("ftc,trc->tfr", picked, values, preferred_element_type=jnp.float32)
         target = (
             (slots // col_tiles)[:, None] == jnp.arange(row_tiles, dtype=jnp.int32)[None, :]
@@ -342,7 +365,7 @@
     def backward_add_group(group_idx, running):
         first_tile = group_idx * 8
         is_live = first_tile + jnp.arange(8, dtype=jnp.int32) < live_count
-        picked = jnp.take(blocks, slots // col_tiles, axis=1)
+        picked = pick_blocks(blocks, slots // col_tiles)
         products = jnp.einsum("ftr,trc->tfc", picked, values, preferred_element_type=jnp.float32)
         target = (
             (slots % col_tiles)[:, None] == jnp.arange(col_tiles, dtype=jnp.int32)[None, :]

time: 93.2 us -> 81.4 us (0.87)
  the two profiles are of different devices: /device:TPU:25 before, /device:TPU:1 now
where the time goes in v2:
time: 81.4 us; the launch traced here: 81.2 us
  Pallas kernels  76 us (93%)
  local copies, waits for them, and re-layouts  3.9 us (5%)
  between operations  1.3 us (2%)
    pallas_call x1, Pallas kernels, fused_device(): pl.pallas_call(functools.partial(fused, R, C, T), out_shape=(jax.ShapeDty...  76 us
    unnamed x5, local copies, waits for them, and re-layouts  3.9 us

profile of v2, /device:TPU:1, one launch (start us, length us, event | category | flops | bytes accessed | tf_op | source)
XLA Modules:
  0.0 81.2 jit_solution(8242121744320220229)
XLA Ops:
  1.3 76.0 %shard_map.85 = (bf16[128,1024]{1,0:T(8,128)(2,1)}, f32[64,128]{1,0:T(8,128)}, f32[64,2048]{1,0:T(8,128)}) custom-call(bf16[64,2048]{1,0:T(8,128)(2,1)} %x_hbm.1, bf16[512,512]{1,0:T(8,128)(2,1)} %w_hbm.1, bf16[1024,128]{1,0:T(8,128)(2,1)} %bitcast.1, s32[1,1,8]{2,1,0:T(1,128)} %slots_ref.1, s32[1,1]{1,0:T(1,128)S(6)} %copy.12.count_ref, ...), custom_call_target="tpu_custom_call" | custom-call | tf_op jit(solution)/shard_map/pallas_call | solution.py:302
  77.2 0.0 copy-start
  77.3 1.7 %copy.13 = bf16[128,1024]{1,0:T(8,128)(2,1)} copy(bf16[128,1024]{1,0:T(8,128)(2,1)} %get-tuple-element.6) | data formatting | bytes 524288
  79.0 1.4 %copy.14 = f32[64,128]{1,0:T(8,128)} copy(f32[64,128]{1,0:T(8,128)} %get-tuple-element.7) | data formatting | bytes 65536
  80.4 0.0 copy-done
  80.4 0.8 copy.15
Async XLA Ops:
  77.2 3.1 %copy-start = (f32[64,2048]{1,0:T(8,128)S(1)}, f32[64,2048]{1,0:T(8,128)}, u32[]{:S(2)}) copy-start(f32[64,2048]{1,0:T(8,128)} %get-tuple-element.8) | copy-start | bytes 1572868

commit v3 on v2

--- a/solution.py
+++ b/solution.py
@@ -15,7 +15,7 @@
     x_ref, w_ref, go_ref, lsem,
     tv_all, xf, pout, prx, agg_s, agg_full, go_full, of_s, of_rx, w_s, w_rx, w2_s, w2_rx,
     ga_s, ga_rx, ga_all,
-    sdir, sfwd, rtv, sgo, rgo, szr, rzr, sa, ra, sof, rof, swz, rwz, swr, rwr, sg, rg, sgz, rgz,
+    sdir, sfwd, rtv, sgo, rgo, szr, rzr, sa, ra, sof, rof, swz, rwz, swr, rwr, sg, rg, sgz, rgz, sgl,
 ):
     L = tv_hbm.shape[1]
     FR, NB = x_ref.shape
@@ -174,6 +174,35 @@
     of_s[...] = (pre * s).astype(BF16).reshape(C, FC, SH)
     ga_rx[mi] = ga_s[mi]
 
+    def hop(q, b, way):
+        sems = sgz if way > 0 else sgl
+        return rcopy(ga_all.at[q, b], ga_all.at[q, b], sems.at[b, q], rgz.at[b, q], colp(mj + way))
+
+    def pass_on(q, b):
+        @pl.when((q <= mj) & (mj < C - 1))
+        def _():
+            hop(q, b, 1).start()
+
+        @pl.when((q >= mj) & (mj > 0))
+        def _():
+            hop(q, b, -1).start()
+
+    def relay(n, carry):
+        b = rows(lax.rem(n, R))
+        d = lax.div(n, R) + 1
+
+        @pl.when(mj >= d)
+        def _():
+            hop(mj - d, b, -1).wait_recv()
+            pass_on(mj - d, b)
+
+        @pl.when(mj + d < C)
+        def _():
+            hop(mj + d, b, 1).wait_recv()
+            pass_on(mj + d, b)
+
+        return carry
+
     def spread(n, carry):
         p = rows(n)
 
@@ -181,9 +210,8 @@
         def _():
             rcopy(ga_s.at[p], ga_rx.at[p], sg.at[p], rg.at[p], rowp(p)).wait_recv()
 
-        for d in range(1, C):
-            rcopy(ga_rx.at[p], ga_all.at[mj, p], sgz.at[p, d], rgz.at[p, mj], colp(cols(d))).start()
         ga_all[mj, p] = ga_rx[p]
+        pass_on(mj, p)
         return carry
 
     lax.fori_loop(0, R, spread, 0)
@@ -213,10 +241,8 @@
     gi_ref[...] = jnp.zeros_like(gi_ref)
 
     def backward(n, carry):
+        relay(n + R * (C - 2), carry)
         b = rows(n)
-        for d in range(1, C):
-            q = cols(d)
-            rcopy(ga_rx.at[b], ga_all.at[q, b], sgz.at[b, d], rgz.at[b, q], colp(q)).wait_recv()
         info = tv_all[b, T * L : T * L + 2 * T, :].astype(F32)
         prods = []
         for t in range(T):
@@ -236,6 +262,7 @@
             gi_ref[:, c * L : (c + 1) * L] = acc
         return carry
 
+    lax.fori_loop(0, R * (C - 2), relay, 0)
     lax.fori_loop(0, R, backward, 0)
 
     for d in range(1, C):
@@ -265,7 +292,15 @@
         for d in range(1, C):
             q = cols(d)
             rcopy(pout.at[q, p], prx.at[mj, p], szr.at[p, d], rzr.at[p, mj], colp(q)).wait_send()
-            rcopy(ga_rx.at[p], ga_all.at[mj, p], sgz.at[p, d], rgz.at[p, mj], colp(q)).wait_send()
+
+        for q in range(C):
+            @pl.when((q <= mj) & (mj < C - 1))
+            def _(q=q):
+                hop(q, p, 1).wait_send()
+
+            @pl.when((q >= mj) & (mj > 0))
+            def _(q=q):
+                hop(q, p, -1).wait_send()
 
         @pl.when(n > 0)
         def _():
@@ -295,7 +330,7 @@
         vm((R, FR, SH), BF16), vm((R, FR, SH), BF16), vm((C, R, FR, SH), BF16),
         dma((R // 2,)), dma((R // 2,)), dma((R,)), dma((C,)), dma((C,)),
         dma((R, C)), dma((R, C)), dma((R,)), dma((R,)), dma((C,)), dma((C,)),
-        dma((C,)), dma((C,)), dma((R,)), dma((R,)), dma((R,)), dma((R,)), dma((R, C)), dma((R, C)),
+        dma((C,)), dma((C,)), dma((R,)), dma((R,)), dma((R,)), dma((R,)), dma((R, C)), dma((R, C)), dma((R, C)),
     ]
     vmem, smem = pl.BlockSpec(memory_space=pltpu.VMEM), pl.BlockSpec(memory_space=pltpu.SMEM)
     hbm = pl.BlockSpec(memory_space=pltpu.HBM)

time: 81.4 us -> 78.2 us (0.961)
  Pallas kernels: 76 us -> 72.8 us
    pallas_call x1, Pallas kernels: 76 us -> 72.8 us  [fused_device(): pl.pallas_call(functools.partial(fused, R, C, T), out_shape=(jax.ShapeDty...]
where the time goes in v3:
time: 78.2 us; the launch traced here: 78 us
  Pallas kernels  72.8 us (93%)
  local copies, waits for them, and re-layouts  3.9 us (5%)
  between operations  1.3 us (2%)
    pallas_call x1, Pallas kernels, fused_device(): pl.pallas_call(functools.partial(fused, R, C, T), out_shape=(jax.ShapeDty...  72.8 us
    unnamed x5, local copies, waits for them, and re-layouts  3.9 us

profile of v3, /device:TPU:1, one launch (start us, length us, event | category | flops | bytes accessed | tf_op | source)
XLA Modules:
  0.0 78.0 jit_solution(1323722391914818326)
XLA Ops:
  1.3 72.8 %shard_map.85 = (bf16[128,1024]{1,0:T(8,128)(2,1)}, f32[64,128]{1,0:T(8,128)}, f32[64,2048]{1,0:T(8,128)}) custom-call(bf16[64,2048]{1,0:T(8,128)(2,1)} %x_hbm.1, bf16[512,512]{1,0:T(8,128)(2,1)} %w_hbm.1, bf16[1024,128]{1,0:T(8,128)(2,1)} %bitcast.1, s32[1,1,8]{2,1,0:T(1,128)} %slots_ref.1, s32[1,1]{1,0:T(1,128)S(6)} %copy.12.count_ref, ...), custom_call_target="tpu_custom_call" | custom-call | tf_op jit(solution)/shard_map/pallas_call | solution.py:337
  74.1 0.0 copy-start
  74.1 1.7 %copy.13 = bf16[128,1024]{1,0:T(8,128)(2,1)} copy(bf16[128,1024]{1,0:T(8,128)(2,1)} %get-tuple-element.6) | data formatting | bytes 524288
  75.8 1.4 %copy.14 = f32[64,128]{1,0:T(8,128)} copy(f32[64,128]{1,0:T(8,128)} %get-tuple-element.7) | data formatting | bytes 65536
  77.2 0.0 copy-done
  77.2 0.8 %copy.15 = f32[64,2048]{1,0:T(8,128)} copy(f32[64,2048]{1,0:T(8,128)S(1)} %copy-done) | data formatting | bytes 1048576
Async XLA Ops:
  74.1 3.1 %copy-start = (f32[64,2048]{1,0:T(8,128)S(1)}, f32[64,2048]{1,0:T(8,128)}, u32[]{:S(2)}) copy-start(f32[64,2048]{1,0:T(8,128)} %get-tuple-element.8) | copy-start | bytes 1572868

commit v4 on v3

--- a/solution.py
+++ b/solution.py
@@ -166,12 +166,15 @@
     agg = agg_full[...].reshape(F, SH)
     pre = lax.dot_general(w_ref[...], agg, (((0,), (0,)), ((), ())), preferred_element_type=F32)
     s = 1.0 / (1.0 + jnp.exp(-pre))
+    of_s[...] = (pre * s).astype(BF16).reshape(C, FC, SH)
+    for d in range(1, C):
+        q = cols(d)
+        rcopy(of_s.at[q], of_rx.at[mj], sof.at[d], rof.at[mj], colp(q)).start()
     gp = (go_full[...].reshape(F, SH).astype(F32) * s * (1.0 + pre * (1.0 - s))).astype(BF16)
     ga_s[...] = jnp.dot(w_ref[...], gp, preferred_element_type=F32).astype(BF16).reshape(R, FR, SH)
     for d in range(1, R):
         p = rows(d)
         rcopy(ga_s.at[p], ga_rx.at[mi], sg.at[p], rg.at[mi], rowp(p)).start()
-    of_s[...] = (pre * s).astype(BF16).reshape(C, FC, SH)
     ga_rx[mi] = ga_s[mi]
 
     def hop(q, b, way):
@@ -222,9 +225,6 @@
     for d in range(1, R):
         p = rows(d)
         rcopy(w_s.at[p], w_rx.at[mi], swr.at[p], rwr.at[mi], rowp(p)).start()
-    for d in range(1, C):
-        q = cols(d)
-        rcopy(of_s.at[q], of_rx.at[mj], sof.at[d], rof.at[mj], colp(q)).start()
     of_rx[mj] = of_s[mj]
 
     total = w_s[mi].astype(F32)

time: 78.2 us -> 77.9 us (level)
  no operation moved by 1% of the time
where the time goes in v4:
time: 77.9 us; the launch traced here: 77.7 us
  Pallas kernels  72.5 us (93%)
  local copies, waits for them, and re-layouts  3.9 us (5%)
  between operations  1.3 us (2%)
    pallas_call x1, Pallas kernels, fused_device(): pl.pallas_call(functools.partial(fused, R, C, T), out_shape=(jax.ShapeDty...  72.5 us
    unnamed x5, local copies, waits for them, and re-layouts  3.9 us

profile of v4, /device:TPU:1, one launch (start us, length us, event | category | flops | bytes accessed | tf_op | source)
XLA Modules:
  0.0 77.7 jit_solution(15819628485922000984)
XLA Ops:
  1.3 72.5 %shard_map.85 = (bf16[128,1024]{1,0:T(8,128)(2,1)}, f32[64,128]{1,0:T(8,128)}, f32[64,2048]{1,0:T(8,128)}) custom-call(bf16[64,2048]{1,0:T(8,128)(2,1)} %x_hbm.1, bf16[512,512]{1,0:T(8,128)(2,1)} %w_hbm.1, bf16[1024,128]{1,0:T(8,128)(2,1)} %bitcast.1, s32[1,1,8]{2,1,0:T(1,128)} %slots_ref.1, s32[1,1]{1,0:T(1,128)S(6)} %copy.12.count_ref, ...), custom_call_target="tpu_custom_call" | custom-call | tf_op jit(solution)/shard_map/pallas_call | solution.py:337
  73.8 0.0 copy-start
  73.8 1.7 %copy.13 = bf16[128,1024]{1,0:T(8,128)(2,1)} copy(bf16[128,1024]{1,0:T(8,128)(2,1)} %get-tuple-element.6) | data formatting | bytes 524288
  75.5 1.4 %copy.14 = f32[64,128]{1,0:T(8,128)} copy(f32[64,128]{1,0:T(8,128)} %get-tuple-element.7) | data formatting | bytes 65536
  76.9 0.0 copy-done
  76.9 0.8 %copy.15 = f32[64,2048]{1,0:T(8,128)} copy(f32[64,2048]{1,0:T(8,128)S(1)} %copy-done) | data formatting | bytes 1048576
Async XLA Ops:
  73.8 3.1 %copy-start = (f32[64,2048]{1,0:T(8,128)S(1)}, f32[64,2048]{1,0:T(8,128)}, u32[]{:S(2)}) copy-start(f32[64,2048]{1,0:T(8,128)} %get-tuple-element.8) | copy-start | bytes 1572868
